TPU v7x, 256 devices: a whole 4x4x8 slice. The times are simulated.
256 devices in a mesh: ctx: 32 (over z, x_lo, core), tp: 8 (over x_hi, y).
Axes of the slice: x: 4 (x_hi: 2, x_lo: 2; x = x_hi * 2 + x_lo), y: 4, z: 8, core: 2. Of those that a mesh axis runs over, the one named last changes fastest.
Arguments:
- projected: bfloat16 [8192, 3, 8192], P('ctx', None, 'tp'), may hold values from -6 to 6
- cotangent: bfloat16 [8192, 8192], P('ctx', 'tp')
- short_filter: float32 [7, 3, 8192], P(None, None, 'tp'), may hold values from -2 to 2
- long_filter: float32 [128, 8192], P(None, 'tp'), may hold values from -0.5 to 0.5
Outputs:
- scaled_grad: bfloat16 [8192, 3, 8192], P('ctx', None, 'tp')
- long_grad: float32 [128, 8192], P('ctx', 'tp')
- short_grad: float32 [7, 3, 8192], P(None, None, 'tp')
- grad_scale: float32 [], replicated
All inputs are finite; a program needn't handle non-finite values.
Results may differ from a plain program's by a relative error of at most 0.0017.
Values may be sent and summed in bfloat16 or wider, within the bound.
A program may use at most 128 MiB of HBM per device.

v0:
```python
import functools

import jax
import jax.numpy as jnp
import ml_dtypes
import numpy as np
from jax import lax
from jax.experimental import pallas as pl
from jax.experimental.pallas import tpu as pltpu
from jax.sharding import PartitionSpec as P

EPSILON = 1e-06
FP8_RANGE = 448.0
MESH = pl.DeviceIdType.MESH

SIZE = 416
PAIRS = SIZE // 16
EDGE = 144
NEAR = 16
FAR = 128
POWER = 11
REACH = 2048.0
LEAST = 1e-30
OWN = 240
SPAN = 400
KEEP = 264
GROUP = 256
TILES = GROUP // 128
CHUNK = 48
f32 = jnp.float32
bf16 = jnp.bfloat16


def joined_np(matrix):
    high = matrix.astype(ml_dtypes.bfloat16)
    low = (matrix - high.astype(np.float64)).astype(ml_dtypes.bfloat16)
    return np.concatenate([high, high, low], axis=1)


@functools.lru_cache(None)
def transforms():
    m = np.arange(SIZE)[None, :]
    k = np.arange(SIZE // 2)[:, None]
    re = np.cos(2 * np.pi * ((k * m) % SIZE) / SIZE)
    im = -np.sin(2 * np.pi * ((k * m) % SIZE) / SIZE)
    im[0] = np.cos(np.pi * m[0])
    weight = np.full((SIZE // 2, 1), 2.0 / SIZE)
    weight[0] = 1.0 / SIZE

    def blocks(a, b):
        return np.stack([a.reshape(PAIRS, 8, SIZE), b.reshape(PAIRS, 8, SIZE)], axis=1).reshape(SIZE, SIZE)

    ahead = blocks(re, im)
    back = blocks(re * weight, im * weight).T
    c = np.arange(128)
    core, x, z, r = c // 64, (c // 32) % 2, (c // 4) % 8, c % 4
    lag = 128 - ((z * 4 + x * 2 + core) * 4 + r)
    return (
        joined_np(ahead[:, :128]),
        joined_np(ahead[:, EDGE : EDGE + OWN]),
        joined_np(ahead[:, NEAR : NEAR + OWN]),
        joined_np(np.concatenate([ahead[:, :EDGE], ahead[:, EDGE + OWN : SPAN]], axis=1)),
        joined_np(ahead[:, :NEAR]),
        joined_np(ahead[:, NEAR + OWN : SPAN]),
        joined_np(back[lag]),
        joined_np(back[128 : 128 + KEEP]),
        joined_np(back[:KEEP]),
    )


def split(value):
    high = value.astype(bf16)
    low = (value - high.astype(f32)).astype(bf16)
    return high, low


def coded(value):
    most = jnp.maximum(jnp.max(jnp.abs(value), axis=0, keepdims=True), LEAST)
    u = value * (REACH / most)
    u2 = u * u
    u4 = u2 * u2
    return ((u4 * u4) * (u2 * u)).astype(bf16), most


def decoded(code, most):
    y = code.astype(f32)
    root = jnp.exp2(jnp.log2(jnp.maximum(jnp.abs(y), 1.2e-38)) * (1.0 / POWER))
    return jnp.where(y < 0, -root, root) * (most * (1.0 / REACH))


def dot(a, b):
    return lax.dot_general(a, b, (((1,), (0,)), ((), ())), preferred_element_type=f32)


def main_kernel(
    x_hbm, g_hbm, sf_hbm, lf_hbm, fh_h, fp_h, fd_h, fph_h, fdn_h, fda_h, bl_h, bf_h, bd_h,
    din, lout, sout, pout,
    x_own, g_own, tail, head, ghead, pcode, dcode, pmost, dmost, pmine, dmine, pmm, dmm, pf, dfil, sf, lf, fh, fp, fd, fph, fdn, fda, bl, bf, bd,
    xs, gs, kf, vf, sp, sd, sh, hi, lo, sx, fil, dpr, df,
    lgs, sgs, lb1, sb1, lb2, sh1, sh2, zsrc, zbuf, pbuf1, pbuf2, pbuf3, pone, ptwo, pthree,
    loads, own, raw_s, raw_r, halo_s, halo_r, core_s, core_r, x_s, x_r, z_s, z_r, epi_s, epi_r,
):
    me = lax.axis_index("ctx")
    count = lax.axis_size("ctx")
    tp = lax.axis_index("tp")
    after = {"ctx": lax.rem(me + 1, count)}
    before = {"ctx": lax.rem(me + count - 1, count)}
    core = lax.rem(me, 2)
    x = lax.rem(me // 2, 2)
    z = me // 4
    hx = tp // 4
    y = lax.rem(tp, 4)
    rows = x_hbm.shape[1]
    groups = x_own.shape[0]

    def at(zz, xx, cc, hh, yy):
        return {"ctx": zz * 4 + xx * 2 + cc, "tp": hh * 4 + yy}

    pair = at(z, x, 1 - core, hx, y)
    cross = at(z, 1 - x, core, hx, y)
    diagonal = at(z, 1 - x, 1 - core, hx, y)
    rings = [at(lax.rem(z + n, 8), x, core, hx, y) for n in range(1, 8)]
    columns = [at(z, x, core, hx, lax.rem(y + n, 4)) for n in range(1, 4)]
    line = [at(z, (x + n // 2) % 2, (core + n) % 2, (hx + n // 4) % 2, y) for n in range(1, 8)]
    barrier = pltpu.get_barrier_semaphore()
    for other in [*rings, after, before, *columns, *line]:
        pl.semaphore_signal(barrier, inc=1, device_id=other, device_id_type=MESH)

    def lanes_of(i):
        return pl.ds(pl.multiple_of(i * GROUP, GROUP), GROUP)

    def own_copies(i):
        return (
            pltpu.make_async_copy(x_hbm.at[:, :, lanes_of(i)], x_own.at[i], own.at[0, i]),
            pltpu.make_async_copy(g_hbm.at[:, lanes_of(i)], g_own.at[i], own.at[1, i]),
        )

    def remote(source, target, send, recv, other):
        return pltpu.make_async_remote_copy(
            src_ref=source, dst_ref=target, send_sem=send, recv_sem=recv, device_id=other, device_id_type=MESH
        )

    def raw_copies():
        plan = (
            (x_hbm.at[:, pl.ds(rows - NEAR, NEAR)], tail, after),
            (x_hbm.at[:, pl.ds(0, NEAR)], head, before),
            (g_hbm.at[pl.ds(0, NEAR)], ghead, before),
        )
        return [remote(a, b, raw_s.at[n], raw_r.at[n], other) for n, (a, b, other) in enumerate(plan)]

    def halo_copies(i):
        plan = (
            (pmine, pcode, after),
            (dmine, dcode, before),
            (pmm, pmost, after),
            (dmm, dmost, before),
        )
        return [
            remote(a.at[i], b.at[i], halo_s.at[n, i], halo_r.at[n, i], other) for n, (a, b, other) in enumerate(plan)
        ]

    sources = (sf_hbm, lf_hbm, fh_h, fp_h, fd_h, fph_h, fdn_h, fda_h, bl_h, bf_h, bd_h)
    targets = (sf, lf, fh, fp, fd, fph, fdn, fda, bl, bf, bd)
    consts = [pltpu.make_async_copy(a, b, loads.at[n]) for n, (a, b) in enumerate(zip(sources, targets))]
    for copy in consts[:1]:
        copy.start()
    for copy in own_copies(0):
        copy.start()
    for copy in consts[1:5]:
        copy.start()
    for i in range(1, groups):
        for copy in own_copies(i):
            copy.start()
    for copy in consts[5:]:
        copy.start()
    for copy in consts[:5]:
        copy.wait()
    inner = (me > 0).astype(f32)
    outer = (me < count - 1).astype(f32)

    def lanes_t(t):
        return pl.ds(128 * t, 128)

    def taps(i, t):
        lanes = pl.ds(pl.multiple_of(i * GROUP + 128 * t, 128), 128)
        return lambda s, n: sf[s, n : n + 1, lanes]

    def feature(i, t, s, start, size, tap):
        total = None
        for n in range(7):
            term = xs[i, s, t, pl.ds(start + NEAR - n, size), :] * tap(s, n)
            total = term if total is None else total + term
        return total

    def features(i, t, q_start, kv_start, size, p_slot, p_row, d_slot, d_row, tap, own_rows=False):
        lanes = pl.ds(128 * t, 128)
        key = feature(i, t, 1, kv_start, size, tap)
        value = feature(i, t, 2, kv_start, size, tap)
        kf[i, t, pl.ds(kv_start, size), :] = key
        vf[i, t, pl.ds(kv_start, size), :] = value
        product = key * value
        if own_rows:
            pf[t, pl.ds(p_row, size), :] = product
        high, low = split(product)
        hi[p_slot, pl.ds(p_row, size), lanes] = high
        lo[p_slot, pl.ds(p_row, size), lanes] = low
        query = feature(i, t, 0, q_start, size, tap)
        gradient = query * gs[i, t, pl.ds(q_start, size), :]
        if own_rows:
            dfil[t, pl.ds(d_row, size), :] = gradient
        high, low = split(gradient)
        hi[d_slot, pl.ds(d_row, size), lanes] = high
        lo[d_slot, pl.ds(d_row, size), lanes] = low

    def taken(slot, size):
        high = hi[slot, 0:size, :]
        return jnp.concatenate([high, lo[slot, 0:size, :], high], axis=0)

    def put(slot, start, value):
        high, low = split(value)
        hi[slot, start : start + value.shape[0], :] = high
        lo[slot, start : start + value.shape[0], :] = low

    def local(i, _, send=True):
        for copy in own_copies(i):
            copy.wait()
        for t in range(TILES):
            lanes = pl.ds(128 * t, 128)
            xs[i, 0, t, NEAR : NEAR + 256] = x_own[i, 0, :, lanes].astype(f32)
            for s in (1, 2):
                xs[i, s, t, EDGE : EDGE + 256] = x_own[i, s, :, lanes].astype(f32)
            gs[i, t, 0:256] = g_own[i, :, lanes].astype(f32)
        for b in range(8):
            put(2, 16 * b, lf[16 * b : 16 * b + 16, lanes_of(i)])
        sh[i] = dot(fh[...], taken(2, 128))
        for t in range(TILES):
            tap = taps(i, t)

            def step(c, _, t=t, tap=tap):
                row = pl.multiple_of(c * CHUNK, 16)
                features(i, t, NEAR + row, EDGE + row, CHUNK, 0, row, 1, row, tap, True)
                return 0

            lax.fori_loop(0, OWN // CHUNK, step, 0)
            pmine[i, :, lanes_t(t)], pmm[i, :, lanes_t(t)] = coded(pf[t, OWN - FAR : OWN, :])
            dmine[i, :, lanes_t(t)], dmm[i, :, lanes_t(t)] = coded(dfil[t, 0:FAR, :])
        if send:
            for copy in halo_copies(i):
                copy.start()
        sp[i] = dot(fp[...], taken(0, OWN))
        sd[i] = dot(fd[...], taken(1, OWN))
        return 0

    local(0, 0, False)
    pl.semaphore_wait(barrier, 19)
    for copy in raw_copies():
        copy.start()
    for copy in halo_copies(0):
        copy.start()
    lax.fori_loop(1, groups, local, 0)
    for copy in raw_copies():
        copy.wait()
    for copy in consts[5:]:
        copy.wait()

    def core_copies(i):
        return (
            remote(
                lgs.at[i, pl.ds(pl.multiple_of((1 - core) * 64, 64), 64)], lb1.at[i], core_s.at[0, i], core_r.at[0, i], pair
            ),
            remote(sgs.at[i, 1 - core], sb1.at[i], core_s.at[1, i], core_r.at[1, i], pair),
        )

    def x_copies(i):
        return (
            remote(lb1.at[i, pl.ds(pl.multiple_of((1 - x) * 32, 32), 32)], lb2.at[i], x_s.at[0, i], x_r.at[0, i], cross),
            remote(sh1.at[i, 1 - x], sh2.at[i], x_s.at[1, i], x_r.at[1, i], cross),
        )

    def z_copies(i):
        return [
            remote(zsrc.at[i, lax.rem(z + n + 1, 8)], zbuf.at[i, n], z_s.at[i, n], z_r.at[i, n], rings[n]) for n in range(7)
        ]

    def after_core(i):
        for copy in core_copies(i):
            copy.wait()
        lb1[i] = lb1[i] + lgs[i, pl.ds(pl.multiple_of(core * 64, 64), 64), :]
        both = sb1[i] + sgs[i, core]
        sh1[i, 0] = both[0:12]
        sh1[i, 1] = both[12:24]
        for copy in x_copies(i):
            copy.start()

    def after_x(i):
        for copy in x_copies(i):
            copy.wait()
        total = lb2[i] + lb1[i, pl.ds(pl.multiple_of(x * 32, 32), 32), :]
        short = sh2[i] + sh1[i, x]
        for n in range(8):
            zsrc[i, n, 0:4] = total[4 * n : 4 * n + 4, 0:128]
            zsrc[i, n, 4:8] = total[4 * n : 4 * n + 4, 128:256]
            zsrc[i, n, 8:20] = short
        for copy in z_copies(i):
            copy.start()

    def group(i, top):
        for copy in halo_copies(i):
            copy.wait_recv()
        for t in range(TILES):
            wide = pl.ds(pl.multiple_of(i * GROUP + 128 * t, 128), 128)
            lanes = lanes_t(t)
            tap = taps(i, t)
            xs[i, 0, t, 0:NEAR] = tail[0, :, wide].astype(f32) * inner
            xs[i, 0, t, NEAR + 256 : 2 * NEAR + 256] = head[0, :, wide].astype(f32)
            for s in (1, 2):
                xs[i, s, t, FAR:EDGE] = tail[s, :, wide].astype(f32) * inner
                xs[i, s, t, EDGE + 256 : SIZE] = head[s, :, wide].astype(f32)
            gs[i, t, 256 : 256 + NEAR] = ghead[:, wide].astype(f32) * outer
            for c in range(0, FAR, 32):
                high, low = split(decoded(pcode[i, c : c + 32, lanes], pmost[i, :, lanes] * inner))
                hi[0, c : c + 32, lanes] = high
                lo[0, c : c + 32, lanes] = low
                high, low = split(decoded(dcode[i, c : c + 32, lanes], dmost[i, :, lanes] * outer))
                hi[1, NEAR + c : NEAR + c + 32, lanes] = high
                lo[1, NEAR + c : NEAR + c + 32, lanes] = low
            features(i, t, 0, FAR, NEAR, 0, FAR, 2, 0, tap)
            features(i, t, 256, EDGE + OWN, NEAR, 0, EDGE, 1, 0, tap)
        sp[i] = sp[i] + dot(fph[...], taken(0, EDGE + NEAR))
        sd[i] = sd[i] + dot(fdn[...], taken(2, NEAR))
        sx[...] = sd[i] + dot(fda[...], taken(1, EDGE))

        row = lax.broadcasted_iota(jnp.int32, (8, GROUP), 0)
        for b in range(PAIRS):

            def two(ref, b=b):
                return ref[16 * b : 16 * b + 8, :], ref[16 * b + 8 : 16 * b + 16, :]

            pr, pi = two(sp.at[i])
            hr, him = two(sh.at[i])
            dr, di = two(sd.at[i])
            xr, xi = two(sx)

            def pack(same, cross_, re, im, sign, special=b == 0):
                if special:
                    real = re + sign * jnp.where(row == 0, 0.0, same)
                    imag = jnp.where(row == 0, same, im + cross_)
                else:
                    real = re + same if sign > 0 else re - same
                    imag = im + cross_
                return jnp.concatenate([real, imag], axis=0)

            put(0, 16 * b, pack(di * pi, -(di * pr), dr * pr, dr * pi, 1.0))
            put(1, 16 * b, pack(pi * him, pi * hr, pr * hr, pr * him, -1.0))
            put(2, 16 * b, pack(xi * him, xi * hr, xr * hr, -(xr * him), 1.0))

        lgs[i] = dot(bl[...], taken(0, SIZE))
        fil[...] = dot(bf[...], taken(1, SIZE))
        dpr[...] = dot(bd[...], taken(2, SIZE))

        for t in range(TILES):
            lanes = pl.ds(128 * t, 128)
            df[0, t, 0:KEEP, :] = gs[i, t, 0:KEEP, :] * fil[:, lanes]
            df[1, t, 0:KEEP, :] = dpr[:, lanes] * vf[i, t, 128 : 128 + KEEP, :]
            df[2, t, 0:KEEP, :] = dpr[:, lanes] * kf[i, t, 128 : 128 + KEEP, :]

        for t in range(TILES):
            lanes = pl.ds(128 * t, 128)
            tap = taps(i, t)
            for s in range(3):
                shift = NEAR if s == 0 else EDGE

                def step(c, carry, s=s, t=t, lanes=lanes, shift=shift, tap=tap):
                    top, sums = carry
                    base = pl.multiple_of(c * 64, 8)
                    total = None
                    for n in range(7):
                        term = df[s, t, pl.ds(base + n, 64), :] * tap(s, n)
                        total = term if total is None else total + term
                    din[i, s, pl.ds(base, 64), lanes] = total
                    top = jnp.maximum(top, jnp.max(jnp.abs(total).reshape(8, 8, 128), axis=0))
                    here = df[s, t, pl.ds(base, 64), :]
                    new = []
                    for n in range(7):
                        term = here * xs[i, s, t, pl.ds(base + shift - n, 64), :]
                        new.append(sums[n] + jnp.sum(term.reshape(8, 8, 128), axis=0))
                    return top, tuple(new)

                zero = jnp.zeros((8, 128), f32)
                top, sums = lax.fori_loop(0, 4, step, (top, (zero,) * 7))
                sgs[i, t, 8 * s : 8 * s + 8] = jnp.concatenate(
                    [jnp.sum(v, axis=0, keepdims=True) for v in sums] + [jnp.zeros((1, 128), f32)], axis=0
                )
        for copy in core_copies(i):
            copy.start()

        @pl.when(jnp.logical_and(i > 0, i < groups - 1))
        def _():
            after_core(i - 1)

        @pl.when(jnp.logical_and(i > 1, i < groups - 1))
        def _():
            after_x(i - 2)

        return top

    top = lax.fori_loop(0, groups, group, jnp.zeros((8, 128), f32))

    def spread(source, slots, first, others):
        copies = [remote(source, slots.at[n], epi_s.at[first + n], epi_r.at[first + n], o) for n, o in enumerate(others)]
        for copy in copies:
            copy.start()
        return copies

    def gather(top, copies, slots):
        for copy in copies:
            copy.wait_recv()
        for n in range(len(copies)):
            top = jnp.maximum(top, slots[n])
        return top

    pone[...] = top
    ones = spread(pone, pbuf1, 0, line)
    after_core(groups - 2)
    after_x(groups - 3)
    after_core(groups - 1)
    top = gather(top, ones, pbuf1)
    ptwo[...] = top
    twos = spread(ptwo, pbuf2, 7, columns)
    after_x(groups - 2)
    after_x(groups - 1)
    top = gather(top, twos, pbuf2)
    pthree[...] = top
    threes = spread(pthree, pbuf3, 10, rings)
    for i in range(groups):
        for copy in z_copies(i):
            copy.wait_recv()
        whole = zsrc[i, z]
        for n in range(7):
            whole = whole + zbuf[i, n]
        lout[:, GROUP * i : GROUP * i + 128] = whole[0:4]
        lout[:, GROUP * i + 128 : GROUP * (i + 1)] = whole[4:8]
        sout[core, x, i] = whole[8:20]
    quarter = sout.at[core, x]
    lasts = [
        remote(quarter, quarter, epi_s.at[17 + n], epi_r.at[17 + n], o) for n, o in enumerate((pair, cross, diagonal))
    ]
    for copy in lasts:
        copy.start()
    pout[...] = gather(top, threes, pbuf3)
    for copy in (*ones, *twos, *threes):
        copy.wait_send()
    for i in range(groups):
        for copy in (*halo_copies(i), *z_copies(i)):
            copy.wait_send()
    for copy in lasts:
        copy.wait()


def main(x3, cotangent, sf, lf):
    _, rows, chan = x3.shape
    consts = [jnp.asarray(c) for c in transforms()]
    groups = chan // GROUP
    anywhere = pl.BlockSpec(memory_space=pl.ANY)
    vmem = pl.BlockSpec(memory_space=pltpu.VMEM)
    V = pltpu.VMEM
    D = pltpu.SemaphoreType.DMA
    return pl.pallas_call(
        main_kernel,
        out_shape=[
            V((groups, 3, rows, GROUP), f32),
            jax.ShapeDtypeStruct((4, chan), f32),
            jax.ShapeDtypeStruct((2, 2, groups, 12, 128), f32),
            jax.ShapeDtypeStruct((8, 128), f32),
        ],
        in_specs=[anywhere] * (4 + len(consts)),
        out_specs=[vmem, vmem, vmem, vmem],
        scratch_shapes=[
            V((groups, 3, rows, GROUP), bf16),
            V((groups, rows, GROUP), bf16),
            V((3, NEAR, chan), bf16),
            V((3, NEAR, chan), bf16),
            V((NEAR, chan), bf16),
            V((groups, FAR, GROUP), bf16),
            V((groups, FAR, GROUP), bf16),
            V((groups, 1, GROUP), f32),
            V((groups, 1, GROUP), f32),
            V((groups, FAR, GROUP), bf16),
            V((groups, FAR, GROUP), bf16),
            V((groups, 1, GROUP), f32),
            V((groups, 1, GROUP), f32),
            V((TILES, OWN, 128), f32),
            V((TILES, OWN, 128), f32),
            V(sf.shape, f32),
            V(lf.shape, f32),
            *[V(c.shape, bf16) for c in consts],
            V((groups, 3, TILES, SIZE, 128), f32),
            V((groups, TILES, SPAN, 128), f32),
            V((groups, TILES, SPAN, 128), f32),
            V((groups, TILES, SPAN, 128), f32),
            V((groups, SIZE, GROUP), f32),
            V((groups, SIZE, GROUP), f32),
            V((groups, SIZE, GROUP), f32),
            V((3, SIZE, GROUP), bf16),
            V((3, SIZE, GROUP), bf16),
            V((SIZE, GROUP), f32),
            V((KEEP, GROUP), f32),
            V((KEEP, GROUP), f32),
            V((3, TILES, KEEP + 8, 128), f32),
            V((groups, 128, GROUP), f32),
            V((groups, 2, 24, 128), f32),
            V((groups, 64, GROUP), f32),
            V((groups, 24, 128), f32),
            V((groups, 32, GROUP), f32),
            V((groups, 2, 12, 128), f32),
            V((groups, 12, 128), f32),
            V((groups, 8, 20, 128), f32),
            V((groups, 7, 20, 128), f32),
            V((7, 8, 128), f32),
            V((3, 8, 128), f32),
            V((7, 8, 128), f32),
            V((8, 128), f32),
            V((8, 128), f32),
            V((8, 128), f32),
            D((11,)),
            D((2, groups)),
            D((3,)),
            D((3,)),
            D((4, groups)),
            D((4, groups)),
            D((2, groups)),
            D((2, groups)),
            D((2, groups)),
            D((2, groups)),
            D((groups, 7)),
            D((groups, 7)),
            D((20,)),
            D((20,)),
        ],
        compiler_params=pltpu.CompilerParams(
            collective_id=0, has_side_effects=True, vmem_limit_bytes=56 * 1024 * 1024
        ),
        name="gradients",
    )(x3, cotangent, sf, lf, *consts)


STEPS = 2


def scale_kernel(din, lsum, ssum, peak, out_hbm, lout, sout, scale, out, stores):
    groups, streams, rows, _ = din.shape
    step = rows // STEPS
    top = jnp.max(peak[...]) + EPSILON
    factor = FP8_RANGE / top
    copies = []
    for s in range(streams):
        for n in range(STEPS):
            here = pl.ds(n * step, step)
            for i in range(groups):
                out[s, here, GROUP * i : GROUP * (i + 1)] = (din[i, s, here, :] * factor).astype(bf16)
            copies.append(pltpu.make_async_copy(out.at[s, here], out_hbm.at[s, here], stores.at[s * STEPS + n]))
            copies[-1].start()
    scale[0, 0] = top / FP8_RANGE
    lout[...] = lsum[...]
    for c in range(2):
        for i in range(groups):
            lanes = pl.ds(GROUP * i + 128 * c, 128)
            sout[0, :, lanes] = ssum[c, 0, i, 0:7]
            sout[1, 0:4, lanes] = ssum[c, 0, i, 8:12]
            sout[1, 4:7, lanes] = ssum[c, 1, i, 0:3]
            sout[2, :, lanes] = ssum[c, 1, i, 4:11]
    for copy in copies:
        copy.wait()


def scaled(din, lsum, ssum, peak):
    groups, _, rows, _ = din.shape
    chan = groups * GROUP
    vmem = pl.BlockSpec(memory_space=pltpu.VMEM)
    anywhere = pl.BlockSpec(memory_space=pl.ANY)
    din = pltpu.with_memory_space_constraint(din, pltpu.VMEM)
    return pl.pallas_call(
        scale_kernel,
        out_shape=[
            jax.ShapeDtypeStruct((3, rows, chan), bf16),
            jax.ShapeDtypeStruct((4, chan), f32),
            jax.ShapeDtypeStruct((3, 7, chan), f32),
            jax.ShapeDtypeStruct((1, 1), f32),
        ],
        in_specs=[vmem, vmem, vmem, vmem],
        out_specs=[anywhere, vmem, vmem, pl.BlockSpec(memory_space=pltpu.SMEM)],
        scratch_shapes=[pltpu.VMEM((3, rows, chan), bf16), pltpu.SemaphoreType.DMA((3 * STEPS,))],
        compiler_params=pltpu.CompilerParams(vmem_limit_bytes=32 * 1024 * 1024),
        name="scaling",
    )(din, lsum, ssum, peak)


def body(projected, cotangent, short_filter, long_filter):
    x3 = projected.transpose(1, 0, 2)
    sf = short_filter.transpose(1, 0, 2)
    out, long_grad, short_grad, scale = scaled(*main(x3, cotangent, sf, long_filter))
    return out.transpose(1, 0, 2), long_grad, short_grad.transpose(1, 0, 2), scale.reshape(())


def solution(mesh):
    placed = (P("ctx", None, "tp"), P("ctx", "tp"), P(None, None, "tp"), P(None, "tp"))
    return jax.shard_map(
        body,
        mesh=mesh,
        in_specs=placed,
        out_specs=(P("ctx", None, "tp"), P("ctx", "tp"), P(None, None, "tp"), P()),
        check_vma=False,
    )
```

profile of v0, /device:TPU:1, one launch (start us, length us, event | category | flops | bytes accessed | tf_op | source)
XLA Modules:
  0.0 48.3 jit_solution(8291408824786135183)
XLA Ops:
  0.6 43.4 %gradients.1 = (f32[4,3,256,256]{3,2,1,0:T(8,128)S(1)}, f32[4,1024]{1,0:T(4,128)}, f32[2,2,4,12,128]{4,3,2,1,0:T(8,128)}, f32[8,128]{1,0:T(8,128)}) custom-call(bf16[3,256,1024]{2,1,0:T(8,128)(2,1)} %bitcast.5, bf16[256,1024]{1,0:T(8,128)(2,1)} %g_hbm.1, f32[3,7,1024]{2,1,0:T(8,128)} %bitcast.6, f32[128,1024]{1,0:T(8,128)} %lf_hbm.1, ...), custom_call_target="tpu_custom_call" | custom-call | tf_op jit(solution)/shard_map/gradients/pallas_call | solution.py:468
  44.0 0.0 copy-start
  44.0 0.9 %copy-done = f32[2,2,4,12,128]{4,3,2,1,0:T(8,128)S(1)} copy-done((f32[2,2,4,12,128]{4,3,2,1,0:T(8,128)S(1)}, f32[2,2,4,12,128]{4,3,2,1,0:T(8,128)}, u32[]{:S(2)}) %copy-start) | copy-done | bytes 98328
  44.9 0.0 copy-start.1
  44.9 0.7 %copy-done.1 = f32[4,1024]{1,0:T(4,128)S(1)} copy-done((f32[4,1024]{1,0:T(4,128)S(1)}, f32[4,1024]{1,0:T(4,128)}, u32[]{:S(2)}) %copy-start.1) | copy-done | bytes 16408
  45.6 0.0 copy-start.2
  45.6 0.7 %copy-done.2 = f32[8,128]{1,0:T(8,128)S(1)} copy-done((f32[8,128]{1,0:T(8,128)S(1)}, f32[8,128]{1,0:T(8,128)}, u32[]{:S(2)}) %copy-start.2) | copy-done | bytes 4120
  46.3 2.0 %scaling.1 = (bf16[3,256,1024]{2,1,0:T(8,128)(2,1)}, f32[4,1024]{1,0:T(4,128)}, f32[3,7,1024]{2,1,0:T(8,128)}, f32[1,1]{1,0:T(1,128)}) custom-call(f32[4,3,256,256]{3,2,1,0:T(8,128)S(1)} %get-tuple-element.12.din, f32[4,1024]{1,0:T(4,128)S(1)} %copy-done.1, f32[2,2,4,12,128]{4,3,2,1,0:T(8,128)S(1)} %copy-done, f32[8,128]{1,0:T(8,128)S(1)} %copy-done.2), custom_call_target="tpu_custom_call" | custom-call | tf_op jit(solution)/shard_map/scaling/pallas_call | solution.py:582
Async XLA Ops:
  44.0 0.9 %copy-start = (f32[2,2,4,12,128]{4,3,2,1,0:T(8,128)S(1)}, f32[2,2,4,12,128]{4,3,2,1,0:T(8,128)}, u32[]{:S(2)}) copy-start(f32[2,2,4,12,128]{4,3,2,1,0:T(8,128)} %get-tuple-element.14.ssum) | copy-start | bytes 294916
  44.9 0.7 %copy-start.1 = (f32[4,1024]{1,0:T(4,128)S(1)}, f32[4,1024]{1,0:T(4,128)}, u32[]{:S(2)}) copy-start(f32[4,1024]{1,0:T(4,128)} %get-tuple-element.13.lsum) | copy-start | bytes 49156
  45.6 0.7 %copy-start.2 = (f32[8,128]{1,0:T(8,128)S(1)}, f32[8,128]{1,0:T(8,128)}, u32[]{:S(2)}) copy-start(f32[8,128]{1,0:T(8,128)} %get-tuple-element.15.peak) | copy-start | bytes 12292
where the time goes:
time: 48.6 us; the launch traced here: 48.3 us
  Pallas kernels  45.4 us (93%)
  local copies, waits for them, and re-layouts  2.29 us (5%)
  between operations  0.65 us (1%)
    pallas_call x1, Pallas kernels, main(): pl.pallas_call(main_kernel, out_shape=[V((groups, 3, rows, GROUP), f32),...  43.4 us
    unnamed x6, local copies, waits for them, and re-layouts  2.29 us
    pallas_call x1, Pallas kernels, scaled(): pl.pallas_call(scale_kernel, out_shape=[jax.ShapeDtypeStruct((3, rows, ch...  2.04 us

commit v1 on v0

--- a/solution.py
+++ b/solution.py
@@ -96,9 +96,9 @@
     x_hbm, g_hbm, sf_hbm, lf_hbm, fh_h, fp_h, fd_h, fph_h, fdn_h, fda_h, bl_h, bf_h, bd_h,
     din, lout, sout, pout,
     x_own, g_own, tail, head, ghead, pcode, dcode, pmost, dmost, pmine, dmine, pmm, dmm, pf, dfil, sf, lf, fh, fp, fd, fph, fdn, fda, bl, bf, bd,
-    xs, gs, kf, vf, sp, sd, sh, hi, lo, sx, fil, dpr, df,
-    lgs, sgs, lb1, sb1, lb2, sh1, sh2, zsrc, zbuf, pbuf1, pbuf2, pbuf3, pone, ptwo, pthree,
-    loads, own, raw_s, raw_r, halo_s, halo_r, core_s, core_r, x_s, x_r, z_s, z_r, epi_s, epi_r,
+    xs, gs, kf, vf, sp, sd, sh, ohi, olo, hi, lo, sx, fil, dpr, df,
+    quart, qbuf, zsrc, zbuf, pbuf1, pbuf2, pbuf3, pone, ptwo, pthree,
+    loads, own, raw_s, raw_r, halo_s, halo_r, line_s, line_r, z_s, z_r, epi_s, epi_r,
 ):
     me = lax.axis_index("ctx")
     count = lax.axis_size("ctx")
@@ -194,6 +194,8 @@
 
     def features(i, t, q_start, kv_start, size, p_slot, p_row, d_slot, d_row, tap, own_rows=False):
         lanes = pl.ds(128 * t, 128)
+        p_hi, p_lo = p_slot
+        d_hi, d_lo = d_slot
         key = feature(i, t, 1, kv_start, size, tap)
         value = feature(i, t, 2, kv_start, size, tap)
         kf[i, t, pl.ds(kv_start, size), :] = key
@@ -202,107 +204,106 @@
         if own_rows:
             pf[t, pl.ds(p_row, size), :] = product
         high, low = split(product)
-        hi[p_slot, pl.ds(p_row, size), lanes] = high
-        lo[p_slot, pl.ds(p_row, size), lanes] = low
+        p_hi[pl.ds(p_row, size), lanes] = high
+        p_lo[pl.ds(p_row, size), lanes] = low
         query = feature(i, t, 0, q_start, size, tap)
         gradient = query * gs[i, t, pl.ds(q_start, size), :]
         if own_rows:
             dfil[t, pl.ds(d_row, size), :] = gradient
         high, low = split(gradient)
-        hi[d_slot, pl.ds(d_row, size), lanes] = high
-        lo[d_slot, pl.ds(d_row, size), lanes] = low
+        d_hi[pl.ds(d_row, size), lanes] = high
+        d_lo[pl.ds(d_row, size), lanes] = low
+
+    def at_slot(slot):
+        return hi.at[slot], lo.at[slot]
+
+    def tripled(high, low):
+        return jnp.concatenate([high, low, high], axis=0)
 
     def taken(slot, size):
-        high = hi[slot, 0:size, :]
-        return jnp.concatenate([high, lo[slot, 0:size, :], high], axis=0)
+        return tripled(hi[slot, 0:size, :], lo[slot, 0:size, :])
 
     def put(slot, start, value):
         high, low = split(value)
         hi[slot, start : start + value.shape[0], :] = high
         lo[slot, start : start + value.shape[0], :] = low
 
-    def local(i, _, send=True):
+    def near(i):
         for copy in own_copies(i):
             copy.wait()
         for t in range(TILES):
-            lanes = pl.ds(128 * t, 128)
+            lanes = lanes_t(t)
             xs[i, 0, t, NEAR : NEAR + 256] = x_own[i, 0, :, lanes].astype(f32)
             for s in (1, 2):
                 xs[i, s, t, EDGE : EDGE + 256] = x_own[i, s, :, lanes].astype(f32)
             gs[i, t, 0:256] = g_own[i, :, lanes].astype(f32)
+        product = (ohi.at[i, 0], olo.at[i, 0])
+        gradient = (ohi.at[i, 1], olo.at[i, 1])
+        for t in range(TILES):
+            tap = taps(i, t)
+            for row in range(0, OWN, CHUNK):
+                features(i, t, NEAR + row, EDGE + row, CHUNK, product, row, gradient, row, tap, True)
+            pmine[i, :, lanes_t(t)], pmm[i, :, lanes_t(t)] = coded(pf[t, OWN - FAR : OWN, :])
+            dmine[i, :, lanes_t(t)], dmm[i, :, lanes_t(t)] = coded(dfil[t, 0:FAR, :])
+
+    def spectra(i):
         for b in range(8):
             put(2, 16 * b, lf[16 * b : 16 * b + 16, lanes_of(i)])
         sh[i] = dot(fh[...], taken(2, 128))
-        for t in range(TILES):
-            tap = taps(i, t)
-
-            def step(c, _, t=t, tap=tap):
-                row = pl.multiple_of(c * CHUNK, 16)
-                features(i, t, NEAR + row, EDGE + row, CHUNK, 0, row, 1, row, tap, True)
-                return 0
-
-            lax.fori_loop(0, OWN // CHUNK, step, 0)
-            pmine[i, :, lanes_t(t)], pmm[i, :, lanes_t(t)] = coded(pf[t, OWN - FAR : OWN, :])
-            dmine[i, :, lanes_t(t)], dmm[i, :, lanes_t(t)] = coded(dfil[t, 0:FAR, :])
-        if send:
-            for copy in halo_copies(i):
-                copy.start()
-        sp[i] = dot(fp[...], taken(0, OWN))
-        sd[i] = dot(fd[...], taken(1, OWN))
+        sp[i] = dot(fp[...], tripled(ohi[i, 0], olo[i, 0]))
+        sd[i] = dot(fd[...], tripled(ohi[i, 1], olo[i, 1]))
+
+    def send_halo(i):
+        for copy in halo_copies(i):
+            copy.start()
+
+    def local(i, _):
+        near(i)
+        spectra(i - 1)
+        send_halo(i)
         return 0
 
-    local(0, 0, False)
+    near(0)
+    near(1)
+    spectra(0)
     pl.semaphore_wait(barrier, 19)
     for copy in raw_copies():
         copy.start()
-    for copy in halo_copies(0):
-        copy.start()
-    lax.fori_loop(1, groups, local, 0)
+    send_halo(0)
+    send_halo(1)
+    lax.fori_loop(2, groups, local, 0)
+    spectra(groups - 1)
     for copy in raw_copies():
         copy.wait()
     for copy in consts[5:]:
         copy.wait()
 
-    def core_copies(i):
-        return (
+    mine = core * 2 + x
+    trio = [(at(z, (x + n // 2) % 2, (core + n) % 2, hx, y), (core + n) % 2 * 2 + (x + n // 2) % 2) for n in (1, 2, 3)]
+
+    def line_copies(i):
+        return [
+            remote(quart.at[i, whose], qbuf.at[i, n], line_s.at[i, n], line_r.at[i, n], other)
+            for n, (other, whose) in enumerate(trio)
+        ]
+
+    def z_copies(first, size):
+        here = pl.ds(first, size)
+        return [
             remote(
-                lgs.at[i, pl.ds(pl.multiple_of((1 - core) * 64, 64), 64)], lb1.at[i], core_s.at[0, i], core_r.at[0, i], pair
-            ),
-            remote(sgs.at[i, 1 - core], sb1.at[i], core_s.at[1, i], core_r.at[1, i], pair),
-        )
-
-    def x_copies(i):
-        return (
-            remote(lb1.at[i, pl.ds(pl.multiple_of((1 - x) * 32, 32), 32)], lb2.at[i], x_s.at[0, i], x_r.at[0, i], cross),
-            remote(sh1.at[i, 1 - x], sh2.at[i], x_s.at[1, i], x_r.at[1, i], cross),
-        )
-
-    def z_copies(i):
-        return [
-            remote(zsrc.at[i, lax.rem(z + n + 1, 8)], zbuf.at[i, n], z_s.at[i, n], z_r.at[i, n], rings[n]) for n in range(7)
+                zsrc.at[lax.rem(z + n + 1, 8), here], zbuf.at[n, here], z_s.at[first, n], z_r.at[first, n], rings[n]
+            )
+            for n in range(7)
         ]
 
-    def after_core(i):
-        for copy in core_copies(i):
+    def after_line(i):
+        for copy in line_copies(i):
             copy.wait()
-        lb1[i] = lb1[i] + lgs[i, pl.ds(pl.multiple_of(core * 64, 64), 64), :]
-        both = sb1[i] + sgs[i, core]
-        sh1[i, 0] = both[0:12]
-        sh1[i, 1] = both[12:24]
-        for copy in x_copies(i):
-            copy.start()
-
-    def after_x(i):
-        for copy in x_copies(i):
-            copy.wait()
-        total = lb2[i] + lb1[i, pl.ds(pl.multiple_of(x * 32, 32), 32), :]
-        short = sh2[i] + sh1[i, x]
+        total = quart[i, mine] + qbuf[i, 0] + qbuf[i, 1] + qbuf[i, 2]
         for n in range(8):
-            zsrc[i, n, 0:4] = total[4 * n : 4 * n + 4, 0:128]
-            zsrc[i, n, 4:8] = total[4 * n : 4 * n + 4, 128:256]
-            zsrc[i, n, 8:20] = short
-        for copy in z_copies(i):
-            copy.start()
+            zsrc[n, i, 0:4] = total[4 * n : 4 * n + 4]
+            zsrc[n, i, 4:8] = total[32 + 4 * n : 36 + 4 * n]
+            zsrc[n, i, 8:20] = total[64:76]
 
     def group(i, top):
         for copy in halo_copies(i):
@@ -324,8 +325,8 @@
                 high, low = split(decoded(dcode[i, c : c + 32, lanes], dmost[i, :, lanes] * outer))
                 hi[1, NEAR + c : NEAR + c + 32, lanes] = high
                 lo[1, NEAR + c : NEAR + c + 32, lanes] = low
-            features(i, t, 0, FAR, NEAR, 0, FAR, 2, 0, tap)
-            features(i, t, 256, EDGE + OWN, NEAR, 0, EDGE, 1, 0, tap)
+            features(i, t, 0, FAR, NEAR, at_slot(0), FAR, at_slot(2), 0, tap)
+            features(i, t, 256, EDGE + OWN, NEAR, at_slot(0), EDGE, at_slot(1), 0, tap)
         sp[i] = sp[i] + dot(fph[...], taken(0, EDGE + NEAR))
         sd[i] = sd[i] + dot(fdn[...], taken(2, NEAR))
         sx[...] = sd[i] + dot(fda[...], taken(1, EDGE))
@@ -354,7 +355,10 @@
             put(1, 16 * b, pack(pi * him, pi * hr, pr * hr, pr * him, -1.0))
             put(2, 16 * b, pack(xi * him, xi * hr, xr * hr, -(xr * him), 1.0))
 
-        lgs[i] = dot(bl[...], taken(0, SIZE))
+        long_sum = dot(bl[...], taken(0, SIZE))
+        for n in range(4):
+            for t in range(TILES):
+                quart[i, n, 32 * t : 32 * t + 32] = long_sum[32 * n : 32 * n + 32, 128 * t : 128 * t + 128]
         fil[...] = dot(bf[...], taken(1, SIZE))
         dpr[...] = dot(bd[...], taken(2, SIZE))
 
@@ -365,43 +369,41 @@
             df[2, t, 0:KEEP, :] = dpr[:, lanes] * kf[i, t, 128 : 128 + KEEP, :]
 
         for t in range(TILES):
-            lanes = pl.ds(128 * t, 128)
+            short = []
+            for s in range(3):
+                shift = NEAR if s == 0 else EDGE
+                sums = [jnp.zeros((8, 128), f32)] * 7
+                for base in range(0, 256, 64):
+                    here = df[s, t, pl.ds(base, 64), :]
+                    for n in range(7):
+                        term = here * xs[i, s, t, pl.ds(base + shift - n, 64), :]
+                        sums[n] = sums[n] + jnp.sum(term.reshape(8, 8, 128), axis=0)
+                short += [jnp.sum(v, axis=0, keepdims=True) for v in sums] + [jnp.zeros((1, 128), f32)]
+            quart[i, 2 * t, 64:76] = jnp.concatenate(short[:12], axis=0)
+            quart[i, 2 * t + 1, 64:76] = jnp.concatenate(short[12:], axis=0)
+        for copy in line_copies(i):
+            copy.start()
+
+        @pl.when(i > 0)
+        def _():
+            after_line(i - 1)
+
+        @pl.when(i == groups - 1)
+        def _():
+            for copy in z_copies(0, groups - 1):
+                copy.start()
+
+        for t in range(TILES):
+            lanes = lanes_t(t)
             tap = taps(i, t)
             for s in range(3):
-                shift = NEAR if s == 0 else EDGE
-
-                def step(c, carry, s=s, t=t, lanes=lanes, shift=shift, tap=tap):
-                    top, sums = carry
-                    base = pl.multiple_of(c * 64, 8)
+                for base in range(0, 256, 64):
                     total = None
                     for n in range(7):
                         term = df[s, t, pl.ds(base + n, 64), :] * tap(s, n)
                         total = term if total is None else total + term
                     din[i, s, pl.ds(base, 64), lanes] = total
                     top = jnp.maximum(top, jnp.max(jnp.abs(total).reshape(8, 8, 128), axis=0))
-                    here = df[s, t, pl.ds(base, 64), :]
-                    new = []
-                    for n in range(7):
-                        term = here * xs[i, s, t, pl.ds(base + shift - n, 64), :]
-                        new.append(sums[n] + jnp.sum(term.reshape(8, 8, 128), axis=0))
-                    return top, tuple(new)
-
-                zero = jnp.zeros((8, 128), f32)
-                top, sums = lax.fori_loop(0, 4, step, (top, (zero,) * 7))
-                sgs[i, t, 8 * s : 8 * s + 8] = jnp.concatenate(
-                    [jnp.sum(v, axis=0, keepdims=True) for v in sums] + [jnp.zeros((1, 128), f32)], axis=0
-                )
-        for copy in core_copies(i):
-            copy.start()
-
-        @pl.when(jnp.logical_and(i > 0, i < groups - 1))
-        def _():
-            after_core(i - 1)
-
-        @pl.when(jnp.logical_and(i > 1, i < groups - 1))
-        def _():
-            after_x(i - 2)
-
         return top
 
     top = lax.fori_loop(0, groups, group, jnp.zeros((8, 128), f32))
@@ -421,26 +423,26 @@
 
     pone[...] = top
     ones = spread(pone, pbuf1, 0, line)
-    after_core(groups - 2)
-    after_x(groups - 3)
-    after_core(groups - 1)
+    after_line(groups - 1)
+    lasts_z = z_copies(groups - 1, 1)
+    for copy in lasts_z:
+        copy.start()
+    zs = (*z_copies(0, groups - 1), *lasts_z)
     top = gather(top, ones, pbuf1)
     ptwo[...] = top
     twos = spread(ptwo, pbuf2, 7, columns)
-    after_x(groups - 2)
-    after_x(groups - 1)
     top = gather(top, twos, pbuf2)
     pthree[...] = top
     threes = spread(pthree, pbuf3, 10, rings)
+    for copy in zs:
+        copy.wait_recv()
+    whole = zsrc[z]
+    for n in range(7):
+        whole = whole + zbuf[n]
     for i in range(groups):
-        for copy in z_copies(i):
-            copy.wait_recv()
-        whole = zsrc[i, z]
-        for n in range(7):
-            whole = whole + zbuf[i, n]
-        lout[:, GROUP * i : GROUP * i + 128] = whole[0:4]
-        lout[:, GROUP * i + 128 : GROUP * (i + 1)] = whole[4:8]
-        sout[core, x, i] = whole[8:20]
+        lout[:, GROUP * i : GROUP * i + 128] = whole[i, 0:4]
+        lout[:, GROUP * i + 128 : GROUP * (i + 1)] = whole[i, 4:8]
+    sout[core, x] = whole[:, 8:20]
     quarter = sout.at[core, x]
     lasts = [
         remote(quarter, quarter, epi_s.at[17 + n], epi_r.at[17 + n], o) for n, o in enumerate((pair, cross, diagonal))
@@ -448,10 +450,10 @@
     for copy in lasts:
         copy.start()
     pout[...] = gather(top, threes, pbuf3)
-    for copy in (*ones, *twos, *threes):
+    for copy in (*ones, *twos, *threes, *zs):
         copy.wait_send()
     for i in range(groups):
-        for copy in (*halo_copies(i), *z_copies(i)):
+        for copy in halo_copies(i):
             copy.wait_send()
     for copy in lasts:
         copy.wait()
@@ -469,9 +471,9 @@
         main_kernel,
         out_shape=[
             V((groups, 3, rows, GROUP), f32),
-            jax.ShapeDtypeStruct((4, chan), f32),
-            jax.ShapeDtypeStruct((2, 2, groups, 12, 128), f32),
-            jax.ShapeDtypeStruct((8, 128), f32),
+            V((4, chan), f32),
+            V((2, 2, groups, 12, 128), f32),
+            V((8, 128), f32),
         ],
         in_specs=[anywhere] * (4 + len(consts)),
         out_specs=[vmem, vmem, vmem, vmem],
@@ -501,21 +503,18 @@
             V((groups, SIZE, GROUP), f32),
             V((groups, SIZE, GROUP), f32),
             V((groups, SIZE, GROUP), f32),
+            V((groups, 2, OWN, GROUP), bf16),
+            V((groups, 2, OWN, GROUP), bf16),
             V((3, SIZE, GROUP), bf16),
             V((3, SIZE, GROUP), bf16),
             V((SIZE, GROUP), f32),
             V((KEEP, GROUP), f32),
             V((KEEP, GROUP), f32),
             V((3, TILES, KEEP + 8, 128), f32),
-            V((groups, 128, GROUP), f32),
-            V((groups, 2, 24, 128), f32),
-            V((groups, 64, GROUP), f32),
-            V((groups, 24, 128), f32),
-            V((groups, 32, GROUP), f32),
-            V((groups, 2, 12, 128), f32),
-            V((groups, 12, 128), f32),
-            V((groups, 8, 20, 128), f32),
-            V((groups, 7, 20, 128), f32),
+            V((groups, 4, 76, 128), f32),
+            V((groups, 3, 76, 128), f32),
+            V((8, groups, 20, 128), f32),
+            V((7, groups, 20, 128), f32),
             V((7, 8, 128), f32),
             V((3, 8, 128), f32),
             V((7, 8, 128), f32),
@@ -528,17 +527,15 @@
             D((3,)),
             D((4, groups)),
             D((4, groups)),
-            D((2, groups)),
-            D((2, groups)),
-            D((2, groups)),
-            D((2, groups)),
+            D((groups, 3)),
+            D((groups, 3)),
             D((groups, 7)),
             D((groups, 7)),
             D((20,)),
             D((20,)),
         ],
         compiler_params=pltpu.CompilerParams(
-            collective_id=0, has_side_effects=True, vmem_limit_bytes=56 * 1024 * 1024
+            collective_id=0, has_side_effects=True, vmem_limit_bytes=60 * 1024 * 1024
         ),
         name="gradients",
     )(x3, cotangent, sf, lf, *consts)
@@ -578,7 +575,7 @@
     chan = groups * GROUP
     vmem = pl.BlockSpec(memory_space=pltpu.VMEM)
     anywhere = pl.BlockSpec(memory_space=pl.ANY)
-    din = pltpu.with_memory_space_constraint(din, pltpu.VMEM)
+    din, lsum, ssum, peak = [pltpu.with_memory_space_constraint(a, pltpu.VMEM) for a in (din, lsum, ssum, peak)]
     return pl.pallas_call(
         scale_kernel,
         out_shape=[

time: 48.6 us -> 45.4 us (0.934)
  local copies, waits for them, and re-layouts: 2.29 us -> 0 us
  Pallas kernels: 45.4 us -> 44.7 us
    unnamed x6 -> x0, local copies, waits for them, and re-layouts: 2.29 us -> none
    pallas_call x1, Pallas kernels: 43.4 us -> 42.7 us  [main(): pl.pallas_call(main_kernel, out_shape=[V((groups, 3, rows, GROUP), f32),...]
where the time goes in v1:
time: 45.4 us
  Pallas kernels  44.7 us (98%)
  between operations  0.64 us (1%)
    pallas_call x1, Pallas kernels, main(): pl.pallas_call(main_kernel, out_shape=[V((groups, 3, rows, GROUP), f32),...  42.7 us
    pallas_call x1, Pallas kernels, scaled(): pl.pallas_call(scale_kernel, out_shape=[jax.ShapeDtypeStruct((3, rows, ch...  2.04 us

profile of v1, /device:TPU:1, one launch (start us, length us, event | category | flops | bytes accessed | tf_op | source)
XLA Modules:
  0.0 45.4 jit_solution(8722362754618403203)
XLA Ops:
  0.6 42.7 %gradients.1 = (f32[4,3,256,256]{3,2,1,0:T(8,128)S(1)}, f32[4,1024]{1,0:T(4,128)S(1)}, f32[2,2,4,12,128]{4,3,2,1,0:T(8,128)S(1)}, f32[8,128]{1,0:T(8,128)S(1)}) custom-call(bf16[3,256,1024]{2,1,0:T(8,128)(2,1)} %bitcast.5, bf16[256,1024]{1,0:T(8,128)(2,1)} %g_hbm.1, f32[3,7,1024]{2,1,0:T(8,128)} %bitcast.6, f32[128,1024]{1,0:T(8,128)} %lf_hbm.1, ...), custom_call_target="tpu_custom_call" | custom-call | tf_op jit(solution)/shard_map/gradients/pallas_call | solution.py:470
  43.3 2.0 %scaling.1 = (bf16[3,256,1024]{2,1,0:T(8,128)(2,1)}, f32[4,1024]{1,0:T(4,128)}, f32[3,7,1024]{2,1,0:T(8,128)}, f32[1,1]{1,0:T(1,128)}) custom-call(f32[4,3,256,256]{3,2,1,0:T(8,128)S(1)} %get-tuple-element.12.din, f32[4,1024]{1,0:T(4,128)S(1)} %get-tuple-element.13.lsum, f32[2,2,4,12,128]{4,3,2,1,0:T(8,128)S(1)} %get-tuple-element.14.ssum, ...), custom_call_target="tpu_custom_call" | custom-call | tf_op jit(solution)/shard_map/scaling/pallas_call | solution.py:579

commit v2 on v1

--- a/solution.py
+++ b/solution.py
@@ -18,6 +18,8 @@
 EDGE = 144
 NEAR = 16
 FAR = 128
+AHEAD = FAR + 2 * NEAR
+BACK = FAR + 4 * NEAR
 POWER = 11
 REACH = 2048.0
 LEAST = 1e-30
@@ -75,7 +77,7 @@
 
 
 def coded(value):
-    most = jnp.maximum(jnp.max(jnp.abs(value), axis=0, keepdims=True), LEAST)
+    most = jnp.maximum(jnp.max(jnp.abs(value), axis=0, keepdims=True), LEAST).astype(bf16).astype(f32)
     u = value * (REACH / most)
     u2 = u * u
     u4 = u2 * u2
@@ -95,10 +97,10 @@
 def main_kernel(
     x_hbm, g_hbm, sf_hbm, lf_hbm, fh_h, fp_h, fd_h, fph_h, fdn_h, fda_h, bl_h, bf_h, bd_h,
     din, lout, sout, pout,
-    x_own, g_own, tail, head, ghead, pcode, dcode, pmost, dmost, pmine, dmine, pmm, dmm, pf, dfil, sf, lf, fh, fp, fd, fph, fdn, fda, bl, bf, bd,
+    x_own, g_own, ahead, back, from_before, from_after, pf, dfil, sf, lf, fh, fp, fd, fph, fdn, fda, bl, bf, bd,
     xs, gs, kf, vf, sp, sd, sh, ohi, olo, hi, lo, sx, fil, dpr, df,
     quart, qbuf, zsrc, zbuf, pbuf1, pbuf2, pbuf3, pone, ptwo, pthree,
-    loads, own, raw_s, raw_r, halo_s, halo_r, line_s, line_r, z_s, z_r, epi_s, epi_r,
+    loads, own, halo_s, halo_r, line_s, line_r, z_s, z_r, epi_s, epi_r,
 ):
     me = lax.axis_index("ctx")
     count = lax.axis_size("ctx")
@@ -117,14 +119,9 @@
         return {"ctx": zz * 4 + xx * 2 + cc, "tp": hh * 4 + yy}
 
     pair = at(z, x, 1 - core, hx, y)
-    cross = at(z, 1 - x, core, hx, y)
-    diagonal = at(z, 1 - x, 1 - core, hx, y)
     rings = [at(lax.rem(z + n, 8), x, core, hx, y) for n in range(1, 8)]
     columns = [at(z, x, core, hx, lax.rem(y + n, 4)) for n in range(1, 4)]
     line = [at(z, (x + n // 2) % 2, (core + n) % 2, (hx + n // 4) % 2, y) for n in range(1, 8)]
-    barrier = pltpu.get_barrier_semaphore()
-    for other in [*rings, after, before, *columns, *line]:
-        pl.semaphore_signal(barrier, inc=1, device_id=other, device_id_type=MESH)
 
     def lanes_of(i):
         return pl.ds(pl.multiple_of(i * GROUP, GROUP), GROUP)
@@ -140,24 +137,11 @@
             src_ref=source, dst_ref=target, send_sem=send, recv_sem=recv, device_id=other, device_id_type=MESH
         )
 
-    def raw_copies():
-        plan = (
-            (x_hbm.at[:, pl.ds(rows - NEAR, NEAR)], tail, after),
-            (x_hbm.at[:, pl.ds(0, NEAR)], head, before),
-            (g_hbm.at[pl.ds(0, NEAR)], ghead, before),
+    def halo_copies(i):
+        return (
+            remote(ahead.at[i], from_before.at[i], halo_s.at[0, i], halo_r.at[0, i], after),
+            remote(back.at[i], from_after.at[i], halo_s.at[1, i], halo_r.at[1, i], before),
         )
-        return [remote(a, b, raw_s.at[n], raw_r.at[n], other) for n, (a, b, other) in enumerate(plan)]
-
-    def halo_copies(i):
-        plan = (
-            (pmine, pcode, after),
-            (dmine, dcode, before),
-            (pmm, pmost, after),
-            (dmm, dmost, before),
-        )
-        return [
-            remote(a.at[i], b.at[i], halo_s.at[n, i], halo_r.at[n, i], other) for n, (a, b, other) in enumerate(plan)
-        ]
 
     sources = (sf_hbm, lf_hbm, fh_h, fp_h, fd_h, fph_h, fdn_h, fda_h, bl_h, bf_h, bd_h)
     targets = (sf, lf, fh, fp, fd, fph, fdn, fda, bl, bf, bd)
@@ -166,6 +150,9 @@
         copy.start()
     for copy in own_copies(0):
         copy.start()
+    barrier = pltpu.get_barrier_semaphore()
+    for other in [*rings, after, before, *columns, *line]:
+        pl.semaphore_signal(barrier, inc=1, device_id=other, device_id_type=MESH)
     for copy in consts[1:5]:
         copy.start()
     for i in range(1, groups):
@@ -173,8 +160,7 @@
             copy.start()
     for copy in consts[5:]:
         copy.start()
-    for copy in consts[:5]:
-        copy.wait()
+    consts[0].wait()
     inner = (me > 0).astype(f32)
     outer = (me < count - 1).astype(f32)
 
@@ -243,8 +229,19 @@
             tap = taps(i, t)
             for row in range(0, OWN, CHUNK):
                 features(i, t, NEAR + row, EDGE + row, CHUNK, product, row, gradient, row, tap, True)
-            pmine[i, :, lanes_t(t)], pmm[i, :, lanes_t(t)] = coded(pf[t, OWN - FAR : OWN, :])
-            dmine[i, :, lanes_t(t)], dmm[i, :, lanes_t(t)] = coded(dfil[t, 0:FAR, :])
+            lanes = lanes_t(t)
+            code, most = coded(pf[t, OWN - FAR : OWN, :])
+            ahead[i, 0:FAR, lanes] = code
+            for n, parts in enumerate(((jnp.broadcast_to(most, (8, 128)), xs[i, 0, t, 264:272]), (xs[i, 1, t, 392:400], xs[i, 2, t, 392:400]))):
+                ahead[i, FAR + NEAR * n : FAR + NEAR * (n + 1), lanes] = jnp.concatenate(parts, axis=0).astype(bf16)
+            code, most = coded(dfil[t, 0:FAR, :])
+            back[i, 0:FAR, lanes] = code
+            back[i, FAR : FAR + NEAR, lanes] = x_own[i, 0, 0:NEAR, lanes]
+            back[i, FAR + NEAR : FAR + 2 * NEAR, lanes] = g_own[i, 0:NEAR, lanes]
+            back[i, FAR + 2 * NEAR : FAR + 3 * NEAR, lanes] = jnp.concatenate(
+                [xs[i, 1, t, EDGE : EDGE + 8], xs[i, 2, t, EDGE : EDGE + 8]], axis=0
+            ).astype(bf16)
+            back[i, FAR + 3 * NEAR : BACK, lanes] = jnp.broadcast_to(most, (NEAR, 128)).astype(bf16)
 
     def spectra(i):
         for b in range(8):
@@ -264,17 +261,12 @@
         return 0
 
     near(0)
-    near(1)
-    spectra(0)
     pl.semaphore_wait(barrier, 19)
-    for copy in raw_copies():
-        copy.start()
     send_halo(0)
-    send_halo(1)
-    lax.fori_loop(2, groups, local, 0)
+    for copy in consts[1:5]:
+        copy.wait()
+    lax.fori_loop(1, groups, local, 0)
     spectra(groups - 1)
-    for copy in raw_copies():
-        copy.wait()
     for copy in consts[5:]:
         copy.wait()
 
@@ -303,26 +295,32 @@
         for n in range(8):
             zsrc[n, i, 0:4] = total[4 * n : 4 * n + 4]
             zsrc[n, i, 4:8] = total[32 + 4 * n : 36 + 4 * n]
-            zsrc[n, i, 8:20] = total[64:76]
+            zsrc[n, i, 8:32] = total[64:88]
 
     def group(i, top):
         for copy in halo_copies(i):
             copy.wait_recv()
         for t in range(TILES):
-            wide = pl.ds(pl.multiple_of(i * GROUP + 128 * t, 128), 128)
             lanes = lanes_t(t)
             tap = taps(i, t)
-            xs[i, 0, t, 0:NEAR] = tail[0, :, wide].astype(f32) * inner
-            xs[i, 0, t, NEAR + 256 : 2 * NEAR + 256] = head[0, :, wide].astype(f32)
+            edge = from_before[i, FAR : FAR + NEAR, lanes].astype(f32) * inner
+            pmost = edge[0:1]
+            xs[i, 0, t, 8:NEAR] = edge[8:NEAR]
+            edge = from_before[i, FAR + NEAR : AHEAD, lanes].astype(f32) * inner
+            xs[i, 1, t, FAR + 8 : EDGE] = edge[0:8]
+            xs[i, 2, t, FAR + 8 : EDGE] = edge[8:NEAR]
+            xs[i, 0, t, NEAR + 256 : 2 * NEAR + 256] = from_after[i, FAR : FAR + NEAR, lanes].astype(f32)
+            gs[i, t, 256 : 256 + NEAR] = from_after[i, FAR + NEAR : FAR + 2 * NEAR, lanes].astype(f32) * outer
+            edge = from_after[i, FAR + 2 * NEAR : FAR + 3 * NEAR, lanes].astype(f32)
             for s in (1, 2):
-                xs[i, s, t, FAR:EDGE] = tail[s, :, wide].astype(f32) * inner
-                xs[i, s, t, EDGE + 256 : SIZE] = head[s, :, wide].astype(f32)
-            gs[i, t, 256 : 256 + NEAR] = ghead[:, wide].astype(f32) * outer
+                xs[i, s, t, EDGE + 256 : EDGE + 264] = edge[8 * s - 8 : 8 * s]
+                xs[i, s, t, EDGE + 264 : SIZE] = jnp.zeros((8, 128), f32)
+            dmost = from_after[i, FAR + 3 * NEAR : BACK, lanes].astype(f32)[0:1] * outer
             for c in range(0, FAR, 32):
-                high, low = split(decoded(pcode[i, c : c + 32, lanes], pmost[i, :, lanes] * inner))
+                high, low = split(decoded(from_before[i, c : c + 32, lanes], pmost))
                 hi[0, c : c + 32, lanes] = high
                 lo[0, c : c + 32, lanes] = low
-                high, low = split(decoded(dcode[i, c : c + 32, lanes], dmost[i, :, lanes] * outer))
+                high, low = split(decoded(from_after[i, c : c + 32, lanes], dmost))
                 hi[1, NEAR + c : NEAR + c + 32, lanes] = high
                 lo[1, NEAR + c : NEAR + c + 32, lanes] = low
             features(i, t, 0, FAR, NEAR, at_slot(0), FAR, at_slot(2), 0, tap)
@@ -379,18 +377,18 @@
                         term = here * xs[i, s, t, pl.ds(base + shift - n, 64), :]
                         sums[n] = sums[n] + jnp.sum(term.reshape(8, 8, 128), axis=0)
                 short += [jnp.sum(v, axis=0, keepdims=True) for v in sums] + [jnp.zeros((1, 128), f32)]
-            quart[i, 2 * t, 64:76] = jnp.concatenate(short[:12], axis=0)
-            quart[i, 2 * t + 1, 64:76] = jnp.concatenate(short[12:], axis=0)
+            for n in range(2):
+                quart[i, 2 * t + n, 64:88] = jnp.concatenate(short, axis=0)
         for copy in line_copies(i):
             copy.start()
 
-        @pl.when(i > 0)
+        @pl.when(i > 1)
         def _():
-            after_line(i - 1)
+            after_line(i - 2)
 
         @pl.when(i == groups - 1)
         def _():
-            for copy in z_copies(0, groups - 1):
+            for copy in z_copies(0, groups - 2):
                 copy.start()
 
         for t in range(TILES):
@@ -423,14 +421,16 @@
 
     pone[...] = top
     ones = spread(pone, pbuf1, 0, line)
-    after_line(groups - 1)
-    lasts_z = z_copies(groups - 1, 1)
-    for copy in lasts_z:
+    zs = [*z_copies(0, groups - 2), *z_copies(groups - 2, 1), *z_copies(groups - 1, 1)]
+    after_line(groups - 2)
+    for copy in zs[7:14]:
         copy.start()
-    zs = (*z_copies(0, groups - 1), *lasts_z)
     top = gather(top, ones, pbuf1)
     ptwo[...] = top
     twos = spread(ptwo, pbuf2, 7, columns)
+    after_line(groups - 1)
+    for copy in zs[14:]:
+        copy.start()
     top = gather(top, twos, pbuf2)
     pthree[...] = top
     threes = spread(pthree, pbuf3, 10, rings)
@@ -442,21 +442,16 @@
     for i in range(groups):
         lout[:, GROUP * i : GROUP * i + 128] = whole[i, 0:4]
         lout[:, GROUP * i + 128 : GROUP * (i + 1)] = whole[i, 4:8]
-    sout[core, x] = whole[:, 8:20]
-    quarter = sout.at[core, x]
-    lasts = [
-        remote(quarter, quarter, epi_s.at[17 + n], epi_r.at[17 + n], o) for n, o in enumerate((pair, cross, diagonal))
-    ]
-    for copy in lasts:
-        copy.start()
+    sout[core] = whole[:, 8:32]
+    last = remote(sout.at[core], sout.at[core], epi_s.at[17], epi_r.at[17], pair)
+    last.start()
     pout[...] = gather(top, threes, pbuf3)
     for copy in (*ones, *twos, *threes, *zs):
         copy.wait_send()
     for i in range(groups):
         for copy in halo_copies(i):
             copy.wait_send()
-    for copy in lasts:
-        copy.wait()
+    last.wait()
 
 
 def main(x3, cotangent, sf, lf):
@@ -472,7 +467,7 @@
         out_shape=[
             V((groups, 3, rows, GROUP), f32),
             V((4, chan), f32),
-            V((2, 2, groups, 12, 128), f32),
+            V((2, groups, 24, 128), f32),
             V((8, 128), f32),
         ],
         in_specs=[anywhere] * (4 + len(consts)),
@@ -480,17 +475,10 @@
         scratch_shapes=[
             V((groups, 3, rows, GROUP), bf16),
             V((groups, rows, GROUP), bf16),
-            V((3, NEAR, chan), bf16),
-            V((3, NEAR, chan), bf16),
-            V((NEAR, chan), bf16),
-            V((groups, FAR, GROUP), bf16),
-            V((groups, FAR, GROUP), bf16),
-            V((groups, 1, GROUP), f32),
-            V((groups, 1, GROUP), f32),
-            V((groups, FAR, GROUP), bf16),
-            V((groups, FAR, GROUP), bf16),
-            V((groups, 1, GROUP), f32),
-            V((groups, 1, GROUP), f32),
+            V((groups, AHEAD, GROUP), bf16),
+            V((groups, BACK, GROUP), bf16),
+            V((groups, AHEAD, GROUP), bf16),
+            V((groups, BACK, GROUP), bf16),
             V((TILES, OWN, 128), f32),
             V((TILES, OWN, 128), f32),
             V(sf.shape, f32),
@@ -511,10 +499,10 @@
             V((KEEP, GROUP), f32),
             V((KEEP, GROUP), f32),
             V((3, TILES, KEEP + 8, 128), f32),
-            V((groups, 4, 76, 128), f32),
-            V((groups, 3, 76, 128), f32),
-            V((8, groups, 20, 128), f32),
-            V((7, groups, 20, 128), f32),
+            V((groups, 4, 88, 128), f32),
+            V((groups, 3, 88, 128), f32),
+            V((8, groups, 32, 128), f32),
+            V((7, groups, 32, 128), f32),
             V((7, 8, 128), f32),
             V((3, 8, 128), f32),
             V((7, 8, 128), f32),
@@ -523,16 +511,14 @@
             V((8, 128), f32),
             D((11,)),
             D((2, groups)),
-            D((3,)),
-            D((3,)),
-            D((4, groups)),
-            D((4, groups)),
+            D((2, groups)),
+            D((2, groups)),
             D((groups, 3)),
             D((groups, 3)),
             D((groups, 7)),
             D((groups, 7)),
-            D((20,)),
-            D((20,)),
+            D((18,)),
+            D((18,)),
         ],
         compiler_params=pltpu.CompilerParams(
             collective_id=0, has_side_effects=True, vmem_limit_bytes=60 * 1024 * 1024
@@ -562,10 +548,8 @@
     for c in range(2):
         for i in range(groups):
             lanes = pl.ds(GROUP * i + 128 * c, 128)
-            sout[0, :, lanes] = ssum[c, 0, i, 0:7]
-            sout[1, 0:4, lanes] = ssum[c, 0, i, 8:12]
-            sout[1, 4:7, lanes] = ssum[c, 1, i, 0:3]
-            sout[2, :, lanes] = ssum[c, 1, i, 4:11]
+            for s in range(streams):
+                sout[s, :, lanes] = ssum[c, i, 8 * s : 8 * s + 7]
     for copy in copies:
         copy.wait()
 

time: 45.4 us -> 45.6 us (level)
  no operation moved by 1% of the time
where the time goes in v2:
time: 45.6 us; the launch traced here: 45.5 us
  Pallas kernels  44.9 us (98%)
  between operations  0.64 us (1%)
    pallas_call x1, Pallas kernels, main(): pl.pallas_call(main_kernel, out_shape=[V((groups, 3, rows, GROUP), f32),...  42.8 us
    pallas_call x1, Pallas kernels, scaled(): pl.pallas_call(scale_kernel, out_shape=[jax.ShapeDtypeStruct((3, rows, ch...  2.04 us

profile of v2, /device:TPU:1, one launch (start us, length us, event | category | flops | bytes accessed | tf_op | source)
XLA Modules:
  0.0 45.5 jit_solution(2765298357085708149)
XLA Ops:
  0.6 42.8 %gradients.1 = (f32[4,3,256,256]{3,2,1,0:T(8,128)S(1)}, f32[4,1024]{1,0:T(4,128)S(1)}, f32[2,4,24,128]{3,2,1,0:T(8,128)S(1)}, f32[8,128]{1,0:T(8,128)S(1)}) custom-call(bf16[3,256,1024]{2,1,0:T(8,128)(2,1)} %bitcast.5, bf16[256,1024]{1,0:T(8,128)(2,1)} %g_hbm.1, f32[3,7,1024]{2,1,0:T(8,128)} %bitcast.6, f32[128,1024]{1,0:T(8,128)} %lf_hbm.1, ...), custom_call_target="tpu_custom_call" | custom-call | tf_op jit(solution)/shard_map/gradients/pallas_call | solution.py:465
  43.5 2.0 %scaling.1 = (bf16[3,256,1024]{2,1,0:T(8,128)(2,1)}, f32[4,1024]{1,0:T(4,128)}, f32[3,7,1024]{2,1,0:T(8,128)}, f32[1,1]{1,0:T(1,128)}) custom-call(f32[4,3,256,256]{3,2,1,0:T(8,128)S(1)} %get-tuple-element.12.din, f32[4,1024]{1,0:T(4,128)S(1)} %get-tuple-element.13.lsum, f32[2,4,24,128]{3,2,1,0:T(8,128)S(1)} %get-tuple-element.14.ssum, ...), custom_call_target="tpu_custom_call" | custom-call | tf_op jit(solution)/shard_map/scaling/pallas_call | solution.py:563

commit v3 on v2

--- a/solution.py
+++ b/solution.py
@@ -76,12 +76,17 @@
     return high, low
 
 
-def coded(value):
+def powered(value):
     most = jnp.maximum(jnp.max(jnp.abs(value), axis=0, keepdims=True), LEAST).astype(bf16).astype(f32)
     u = value * (REACH / most)
     u2 = u * u
     u4 = u2 * u2
-    return ((u4 * u4) * (u2 * u)).astype(bf16), most
+    return (u4 * u4) * (u2 * u), most
+
+
+def coded(value):
+    power, most = powered(value)
+    return power.astype(bf16), most
 
 
 def decoded(code, most):
@@ -279,23 +284,22 @@
             for n, (other, whose) in enumerate(trio)
         ]
 
-    def z_copies(first, size):
-        here = pl.ds(first, size)
+    def z_copies(i):
         return [
-            remote(
-                zsrc.at[lax.rem(z + n + 1, 8), here], zbuf.at[n, here], z_s.at[first, n], z_r.at[first, n], rings[n]
-            )
-            for n in range(7)
+            remote(zsrc.at[lax.rem(z + n + 1, 8), i], zbuf.at[n, i], z_s.at[i, n], z_r.at[i, n], rings[n]) for n in range(7)
         ]
 
     def after_line(i):
         for copy in line_copies(i):
             copy.wait()
         total = quart[i, mine] + qbuf[i, 0] + qbuf[i, 1] + qbuf[i, 2]
+        long_power, long_most = powered(total[0:64])
+        short_power, short_most = powered(total[64:88])
+        spot = lax.broadcasted_iota(jnp.int32, (24, 128), 0)
+        short_power = jnp.where(spot == 7, long_most, jnp.where(spot == 15, short_most, short_power))
         for n in range(8):
-            zsrc[n, i, 0:4] = total[4 * n : 4 * n + 4]
-            zsrc[n, i, 4:8] = total[32 + 4 * n : 36 + 4 * n]
-            zsrc[n, i, 8:32] = total[64:88]
+            parts = [long_power[4 * n : 4 * n + 4], long_power[32 + 4 * n : 36 + 4 * n], short_power]
+            zsrc[n, i] = jnp.concatenate(parts, axis=0).astype(bf16)
 
     def group(i, top):
         for copy in halo_copies(i):
@@ -385,10 +389,7 @@
         @pl.when(i > 1)
         def _():
             after_line(i - 2)
-
-        @pl.when(i == groups - 1)
-        def _():
-            for copy in z_copies(0, groups - 2):
+            for copy in z_copies(i - 2):
                 copy.start()
 
         for t in range(TILES):
@@ -420,29 +421,29 @@
         return top
 
     pone[...] = top
-    ones = spread(pone, pbuf1, 0, line)
-    zs = [*z_copies(0, groups - 2), *z_copies(groups - 2, 1), *z_copies(groups - 1, 1)]
-    after_line(groups - 2)
-    for copy in zs[7:14]:
-        copy.start()
+    ones = spread(pone, pbuf1, 0, rings)
+    zs = [copy for i in range(groups) for copy in z_copies(i)]
+    for i in (groups - 2, groups - 1):
+        after_line(i)
+        for copy in zs[7 * i : 7 * i + 7]:
+            copy.start()
     top = gather(top, ones, pbuf1)
     ptwo[...] = top
-    twos = spread(ptwo, pbuf2, 7, columns)
-    after_line(groups - 1)
-    for copy in zs[14:]:
-        copy.start()
+    twos = spread(ptwo, pbuf2, 7, line)
     top = gather(top, twos, pbuf2)
     pthree[...] = top
-    threes = spread(pthree, pbuf3, 10, rings)
+    threes = spread(pthree, pbuf3, 14, columns)
     for copy in zs:
         copy.wait_recv()
-    whole = zsrc[z]
-    for n in range(7):
-        whole = whole + zbuf[n]
     for i in range(groups):
-        lout[:, GROUP * i : GROUP * i + 128] = whole[i, 0:4]
-        lout[:, GROUP * i + 128 : GROUP * (i + 1)] = whole[i, 4:8]
-    sout[core] = whole[:, 8:32]
+        long_sum, short_sum = 0.0, 0.0
+        for n in range(8):
+            block = (zsrc[z, i] if n == 7 else zbuf[n, i]).astype(f32)
+            long_sum = long_sum + decoded(block[0:8], block[15:16])
+            short_sum = short_sum + decoded(block[8:32], block[23:24])
+        lout[:, GROUP * i : GROUP * i + 128] = long_sum[0:4]
+        lout[:, GROUP * i + 128 : GROUP * (i + 1)] = long_sum[4:8]
+        sout[core, i] = short_sum
     last = remote(sout.at[core], sout.at[core], epi_s.at[17], epi_r.at[17], pair)
     last.start()
     pout[...] = gather(top, threes, pbuf3)
@@ -501,11 +502,11 @@
             V((3, TILES, KEEP + 8, 128), f32),
             V((groups, 4, 88, 128), f32),
             V((groups, 3, 88, 128), f32),
-            V((8, groups, 32, 128), f32),
-            V((7, groups, 32, 128), f32),
+            V((8, groups, 32, 128), bf16),
+            V((7, groups, 32, 128), bf16),
+            V((7, 8, 128), f32),
             V((7, 8, 128), f32),
             V((3, 8, 128), f32),
-            V((7, 8, 128), f32),
             V((8, 128), f32),
             V((8, 128), f32),
             V((8, 128), f32),

time: 45.6 us -> 42.1 us (0.923)
  Pallas kernels: 44.9 us -> 41.4 us
    pallas_call x1, Pallas kernels: 42.8 us -> 39.3 us  [main(): pl.pallas_call(main_kernel, out_shape=[V((groups, 3, rows, GROUP), f32),...]
where the time goes in v3:
time: 42.1 us; the launch traced here: 42 us
  Pallas kernels  41.4 us (98%)
  between operations  0.64 us (2%)
    pallas_call x1, Pallas kernels, main(): pl.pallas_call(main_kernel, out_shape=[V((groups, 3, rows, GROUP), f32),...  39.3 us
    pallas_call x1, Pallas kernels, scaled(): pl.pallas_call(scale_kernel, out_shape=[jax.ShapeDtypeStruct((3, rows, ch...  2.04 us

profile of v3, /device:TPU:1, one launch (start us, length us, event | category | flops | bytes accessed | tf_op | source)
XLA Modules:
  0.0 42.0 jit_solution(7490791355317717586)
XLA Ops:
  0.6 39.3 %gradients.1 = (f32[4,3,256,256]{3,2,1,0:T(8,128)S(1)}, f32[4,1024]{1,0:T(4,128)S(1)}, f32[2,4,24,128]{3,2,1,0:T(8,128)S(1)}, f32[8,128]{1,0:T(8,128)S(1)}) custom-call(bf16[3,256,1024]{2,1,0:T(8,128)(2,1)} %bitcast.5, bf16[256,1024]{1,0:T(8,128)(2,1)} %g_hbm.1, f32[3,7,1024]{2,1,0:T(8,128)} %bitcast.6, f32[128,1024]{1,0:T(8,128)} %lf_hbm.1, ...), custom_call_target="tpu_custom_call" | custom-call | tf_op jit(solution)/shard_map/gradients/pallas_call | solution.py:466
  40.0 2.0 %scaling.1 = (bf16[3,256,1024]{2,1,0:T(8,128)(2,1)}, f32[4,1024]{1,0:T(4,128)}, f32[3,7,1024]{2,1,0:T(8,128)}, f32[1,1]{1,0:T(1,128)}) custom-call(f32[4,3,256,256]{3,2,1,0:T(8,128)S(1)} %get-tuple-element.12.din, f32[4,1024]{1,0:T(4,128)S(1)} %get-tuple-element.13.lsum, f32[2,4,24,128]{3,2,1,0:T(8,128)S(1)} %get-tuple-element.14.ssum, ...), custom_call_target="tpu_custom_call" | custom-call | tf_op jit(solution)/shard_map/scaling/pallas_call | solution.py:564

commit v4 on v3

--- a/solution.py
+++ b/solution.py
@@ -276,7 +276,7 @@
         copy.wait()
 
     mine = core * 2 + x
-    trio = [(at(z, (x + n // 2) % 2, (core + n) % 2, hx, y), (core + n) % 2 * 2 + (x + n // 2) % 2) for n in (1, 2, 3)]
+    trio = [(at(z, (x + n // 2) % 2, (core + n) % 2, hx, y), (core + n) % 2 * 2 + (x + n // 2) % 2) for n in (3, 2, 1)]
 
     def line_copies(i):
         return [
@@ -386,12 +386,6 @@
         for copy in line_copies(i):
             copy.start()
 
-        @pl.when(i > 1)
-        def _():
-            after_line(i - 2)
-            for copy in z_copies(i - 2):
-                copy.start()
-
         for t in range(TILES):
             lanes = lanes_t(t)
             tap = taps(i, t)
@@ -423,7 +417,7 @@
     pone[...] = top
     ones = spread(pone, pbuf1, 0, rings)
     zs = [copy for i in range(groups) for copy in z_copies(i)]
-    for i in (groups - 2, groups - 1):
+    for i in range(groups):
         after_line(i)
         for copy in zs[7 * i : 7 * i + 7]:
             copy.start()

time: 42.1 us -> 39.1 us (0.929)
  Pallas kernels: 41.4 us -> 38.4 us
    pallas_call x1, Pallas kernels: 39.3 us -> 36.4 us  [main(): pl.pallas_call(main_kernel, out_shape=[V((groups, 3, rows, GROUP), f32),...]
where the time goes in v4:
time: 39.1 us
  Pallas kernels  38.4 us (98%)
  between operations  0.64 us (2%)
    pallas_call x1, Pallas kernels, main(): pl.pallas_call(main_kernel, out_shape=[V((groups, 3, rows, GROUP), f32),...  36.4 us
    pallas_call x1, Pallas kernels, scaled(): pl.pallas_call(scale_kernel, out_shape=[jax.ShapeDtypeStruct((3, rows, ch...  2.04 us

profile of v4, /device:TPU:1, one launch (start us, length us, event | category | flops | bytes accessed | tf_op | source)
XLA Modules:
  0.0 39.1 jit_solution(5615406891393003758)
XLA Ops:
  0.6 36.4 %gradients.1 = (f32[4,3,256,256]{3,2,1,0:T(8,128)S(1)}, f32[4,1024]{1,0:T(4,128)S(1)}, f32[2,4,24,128]{3,2,1,0:T(8,128)S(1)}, f32[8,128]{1,0:T(8,128)S(1)}) custom-call(bf16[3,256,1024]{2,1,0:T(8,128)(2,1)} %bitcast.5, bf16[256,1024]{1,0:T(8,128)(2,1)} %g_hbm.1, f32[3,7,1024]{2,1,0:T(8,128)} %bitcast.6, f32[128,1024]{1,0:T(8,128)} %lf_hbm.1, ...), custom_call_target="tpu_custom_call" | custom-call | tf_op jit(solution)/shard_map/gradients/pallas_call | solution.py:460
  37.0 2.0 %scaling.1 = (bf16[3,256,1024]{2,1,0:T(8,128)(2,1)}, f32[4,1024]{1,0:T(4,128)}, f32[3,7,1024]{2,1,0:T(8,128)}, f32[1,1]{1,0:T(1,128)}) custom-call(f32[4,3,256,256]{3,2,1,0:T(8,128)S(1)} %get-tuple-element.12.din, f32[4,1024]{1,0:T(4,128)S(1)} %get-tuple-element.13.lsum, f32[2,4,24,128]{3,2,1,0:T(8,128)S(1)} %get-tuple-element.14.ssum, ...), custom_call_target="tpu_custom_call" | custom-call | tf_op jit(solution)/shard_map/scaling/pallas_call | solution.py:558

commit v5 on v4

--- a/solution.py
+++ b/solution.py
@@ -284,9 +284,13 @@
             for n, (other, whose) in enumerate(trio)
         ]
 
-    def z_copies(i):
+    def z_copies(first, size):
+        here = pl.ds(first, size)
         return [
-            remote(zsrc.at[lax.rem(z + n + 1, 8), i], zbuf.at[n, i], z_s.at[i, n], z_r.at[i, n], rings[n]) for n in range(7)
+            remote(
+                zsrc.at[lax.rem(z + n + 1, 8), here], zbuf.at[n, here], z_s.at[first, n], z_r.at[first, n], rings[n]
+            )
+            for n in range(7)
         ]
 
     def after_line(i):
@@ -416,11 +420,12 @@
 
     pone[...] = top
     ones = spread(pone, pbuf1, 0, rings)
-    zs = [copy for i in range(groups) for copy in z_copies(i)]
+    zs = [*z_copies(0, groups - 1), *z_copies(groups - 1, 1)]
     for i in range(groups):
         after_line(i)
-        for copy in zs[7 * i : 7 * i + 7]:
-            copy.start()
+        if i >= groups - 2:
+            for copy in zs[7 * (i - groups + 2) : 7 * (i - groups + 3)]:
+                copy.start()
     top = gather(top, ones, pbuf1)
     ptwo[...] = top
     twos = spread(ptwo, pbuf2, 7, line)

time: 39.1 us -> 40.3 us (1.031)
  Pallas kernels: 38.4 us -> 39.6 us
    pallas_call x1, Pallas kernels: 36.4 us -> 37.5 us  [main(): pl.pallas_call(main_kernel, out_shape=[V((groups, 3, rows, GROUP), f32),...]
where the time goes in v5:
time: 40.3 us; the launch traced here: 40.2 us
  Pallas kernels  39.6 us (98%)
  between operations  0.64 us (2%)
    pallas_call x1, Pallas kernels, main(): pl.pallas_call(main_kernel, out_shape=[V((groups, 3, rows, GROUP), f32),...  37.5 us
    pallas_call x1, Pallas kernels, scaled(): pl.pallas_call(scale_kernel, out_shape=[jax.ShapeDtypeStruct((3, rows, ch...  2.04 us

profile of v5, /device:TPU:1, one launch (start us, length us, event | category | flops | bytes accessed | tf_op | source)
XLA Modules:
  0.0 40.2 jit_solution(10280549643030385287)
XLA Ops:
  0.6 37.5 %gradients.1 = (f32[4,3,256,256]{3,2,1,0:T(8,128)S(1)}, f32[4,1024]{1,0:T(4,128)S(1)}, f32[2,4,24,128]{3,2,1,0:T(8,128)S(1)}, f32[8,128]{1,0:T(8,128)S(1)}) custom-call(bf16[3,256,1024]{2,1,0:T(8,128)(2,1)} %bitcast.5, bf16[256,1024]{1,0:T(8,128)(2,1)} %g_hbm.1, f32[3,7,1024]{2,1,0:T(8,128)} %bitcast.6, f32[128,1024]{1,0:T(8,128)} %lf_hbm.1, ...), custom_call_target="tpu_custom_call" | custom-call | tf_op jit(solution)/shard_map/gradients/pallas_call | solution.py:465
  38.2 2.0 %scaling.1 = (bf16[3,256,1024]{2,1,0:T(8,128)(2,1)}, f32[4,1024]{1,0:T(4,128)}, f32[3,7,1024]{2,1,0:T(8,128)}, f32[1,1]{1,0:T(1,128)}) custom-call(f32[4,3,256,256]{3,2,1,0:T(8,128)S(1)} %get-tuple-element.12.din, f32[4,1024]{1,0:T(4,128)S(1)} %get-tuple-element.13.lsum, f32[2,4,24,128]{3,2,1,0:T(8,128)S(1)} %get-tuple-element.14.ssum, ...), custom_call_target="tpu_custom_call" | custom-call | tf_op jit(solution)/shard_map/scaling/pallas_call | solution.py:563
